TPU v7x, 32 devices: a whole 2x2x4 slice. The times are simulated.
32 devices in a mesh: ens: 2 (over y), seq: 4 (over z), mp: 2 (over x), sub: 2 (over core).
Axes of the slice: x: 2, y: 2, z: 4, core: 2. Of those that a mesh axis runs over, the one named last changes fastest.
Arguments:
- grid_latent: bfloat16 [16384, 1024], P(('ens', 'seq'), ('mp', 'sub')), parts along dimension 0, may hold values from -6 to 6
- grid_count: int32 [8], P(('ens', 'seq')), parts along dimension 0, may hold values from 1024 to 2048, as said below
- hidden_embed: bfloat16 [8192, 1024], P(('ens', 'seq'), ('mp', 'sub')), parts along dimension 0, may hold values from -6 to 6
- enc_src_rows: int32 [8, 32, 128], P(('ens', 'seq')), parts along dimension 0, may hold values from 0 to 2047, as said below
- enc_dst_rows: int32 [8, 32, 128], P(('ens', 'seq')), parts along dimension 0, may hold values from 0 to 1023
- enc_weight: float32 [8, 32, 128], P(('ens', 'seq')), parts along dimension 0, may hold values from 0.25 to 1
- dec_src_rows: int32 [8, 48, 128], P(('ens', 'seq')), parts along dimension 0, may hold values from 0 to 1023
- dec_dst_rows: int32 [8, 48, 128], P(('ens', 'seq')), parts along dimension 0, may hold values from 0 to 2047, as said below
- dec_weight: float32 [8, 48, 128], P(('ens', 'seq')), parts along dimension 0, may hold values from 0.25 to 1
- norm_gain: float32 [1024], replicated, may hold values from 0.1 to 1.9
- w_qkv: bfloat16 [1024, 3072], P(None, ('mp', 'sub'))
- w_out: bfloat16 [1024, 1024], P(('mp', 'sub')), may hold values from -0.1875 to 0.1875
- w_up: bfloat16 [1024, 4096], P(None, ('mp', 'sub')), may hold values from -0.1875 to 0.1875
- up_exp: int32 [4096], P(('mp', 'sub')), may hold values from -1 to 1
- w_down: bfloat16 [4096, 1024], P(('mp', 'sub')), may hold values from -0.09375 to 0.09375
- down_exp: int32 [1024], replicated, may hold values from -1 to 1
Outputs:
- hidden_out: bfloat16 [8192, 1024], P(('ens', 'seq'), ('mp', 'sub')), parts along dimension 0
- grid_out: bfloat16 [16384, 1024], P(('ens', 'seq'), ('mp', 'sub')), parts along dimension 0
There are 2 independent parts, one for each index of `ens`. A program takes and returns all parts, laid end to end along the dimension named above; an argument that names none is the same for every part. Nothing has to cross between parts.
Inputs may be any that keep to these rules, and one draw needn't show every extreme that they name: `grid_count`: each block holds between 1024 and 2048 live grid nodes; some block holds exactly 2048. `enc_src_rows`: each source row is below grid_count of its sending block s. `dec_dst_rows`: each destination row is below grid_count of its receiving block d.
All inputs are finite; a program needn't handle non-finite values.
Results may differ from a plain program's by a relative error of at most 0.013.
Values may be sent and summed in bfloat16 or wider, within the bound.
A program may use at most 128 MiB of HBM per device.

v0:
```python
import jax
import jax.numpy as jnp
from jax import lax
from jax.sharding import PartitionSpec as P

HD = 64
WIN = 512
TILE = 128
ESIDE = 4
DSIDE = 4


def padded(cells, sides, width):
    for axis, dim in sides:
        count = lax.axis_size(axis)
        ends = count - 1
        head = lax.slice_in_dim(cells, 0, width, axis=dim)
        tail = lax.slice_in_dim(cells, cells.shape[dim] - width, cells.shape[dim], axis=dim)
        cells = jnp.concatenate(
            [
                lax.ppermute(tail, axis, [(i, (i + 1) % count) for i in range(ends)]),
                cells,
                lax.ppermute(head, axis, [((i + 1) % count, i) for i in range(ends)]),
            ],
            axis=dim,
        )
    return cells


def normed_rows(rows, norm_gain):
    values = rows.astype(jnp.float32)
    row_mean = jnp.mean(values, axis=-1, keepdims=True)
    centered = values - row_mean
    row_var = jnp.mean(centered * centered, axis=-1, keepdims=True)
    return (centered * lax.rsqrt(row_var + 1e-05) * norm_gain[None, :]).astype(jnp.bfloat16)


def split_heads(normed, w_qkv):
    heads_here = w_qkv.shape[1] // (3 * HD)
    qkv = jnp.dot(normed, w_qkv, preferred_element_type=jnp.float32).reshape(
        normed.shape[0], heads_here, 3, HD
    )
    return qkv.astype(jnp.bfloat16)


def edge_messages(source, src_rows, weights):
    picked = (
        jnp.take(source, src_rows.reshape(-1), axis=0).astype(jnp.float32)
        * weights.reshape(-1)[:, None]
    )
    return picked.astype(jnp.bfloat16)


def arrange_arrivals(messages, extended, width):
    return jnp.concatenate([extended[:width], extended[3 * width :], messages[2 * width :]], axis=0)


def shards(
    grid_latent,
    grid_count,
    hidden_embed,
    enc_src_rows,
    enc_dst_rows,
    enc_weight,
    dec_src_rows,
    dec_dst_rows,
    dec_weight,
    norm_gain,
    w_qkv,
    w_out,
    w_up,
    up_exp,
    w_down,
    down_exp,
):
    blocks = lax.axis_size("seq")
    seq_index = lax.axis_index("seq")
    hid_rows = hidden_embed.shape[0]
    enc_width = ESIDE * TILE
    enc_messages = edge_messages(grid_latent, enc_src_rows, enc_weight)
    enc_extended = padded(enc_messages[: 2 * enc_width], (("seq", 0),), enc_width)
    arrived = arrange_arrivals(enc_messages, enc_extended, enc_width)
    encoded = jax.ops.segment_sum(
        arrived.astype(jnp.float32), enc_dst_rows.reshape(-1), num_segments=hid_rows
    )
    latent = (hidden_embed.astype(jnp.float32) + encoded).astype(jnp.bfloat16)
    heads_here = w_qkv.shape[1] // (3 * HD)
    full_rows = lax.all_gather(latent, ("mp", "sub"), axis=1, tiled=True)
    normed = normed_rows(full_rows, norm_gain)
    qkv = split_heads(normed, w_qkv)
    queries = qkv[:, :, 0, :]
    stacked = qkv[:, :, 1:, :].transpose(0, 2, 1, 3).reshape(hid_rows, 2, heads_here * HD)
    stacked_ext = padded(stacked, (("seq", 0),), WIN)
    stacked_ext = stacked_ext.reshape(hid_rows + 2 * WIN, 2, heads_here, HD)
    keys_ext = stacked_ext[:, 0]
    values_ext = stacked_ext[:, 1]
    query_rows = min(512, hid_rows)
    span = query_rows + 2 * WIN
    hidden_total = hid_rows * blocks
    scale = HD ** (-0.5)
    attended_blocks = []
    for block in range(hid_rows // query_rows):
        first = block * query_rows
        query_block = queries[first : first + query_rows]
        key_block = keys_ext[first : first + span]
        value_block = values_ext[first : first + span]
        scores = (
            jnp.einsum("qhd,khd->hqk", query_block, key_block, preferred_element_type=jnp.float32)
            * scale
        )
        query_pos = seq_index * hid_rows + first + jnp.arange(query_rows, dtype=jnp.int32)
        key_pos = seq_index * hid_rows + first - WIN + jnp.arange(span, dtype=jnp.int32)
        allowed = (
            (jnp.abs(query_pos[:, None] - key_pos[None, :]) <= WIN)
            & (key_pos[None, :] >= 0)
            & (key_pos[None, :] < hidden_total)
        )
        scores = jnp.where(allowed[None, :, :], scores, -1e30)
        peak = jnp.max(scores, axis=-1, keepdims=True)
        expo = jnp.exp(scores - peak)
        attn_weights = (expo / jnp.sum(expo, axis=-1, keepdims=True)).astype(jnp.bfloat16)
        mixed = jnp.einsum(
            "hqk,khd->qhd", attn_weights, value_block, preferred_element_type=jnp.float32
        )
        attended_blocks.append(mixed.astype(jnp.bfloat16).reshape(query_rows, heads_here * HD))
    attended = jnp.concatenate(attended_blocks, axis=0)
    up_proj = (
        jnp.dot(normed, w_up, preferred_element_type=jnp.float32)
        * jnp.exp2(up_exp.astype(jnp.float32))[None, :]
    )
    activated = jax.nn.gelu(up_proj, approximate=False).astype(jnp.bfloat16)
    attn_part = jnp.dot(attended, w_out, preferred_element_type=jnp.float32)
    mlp_part = (
        jnp.dot(activated, w_down, preferred_element_type=jnp.float32)
        * jnp.exp2(down_exp.astype(jnp.float32))[None, :]
    )
    summed = lax.psum_scatter(
        (attn_part + mlp_part).astype(jnp.bfloat16), ("mp", "sub"), scatter_dimension=1, tiled=True
    ).astype(jnp.float32)
    hidden_out = (latent.astype(jnp.float32) + summed).astype(jnp.bfloat16)
    dec_width = DSIDE * TILE
    dec_messages = edge_messages(hidden_out, dec_src_rows, dec_weight)
    dec_extended = padded(dec_messages[: 2 * dec_width], (("seq", 0),), dec_width)
    arrived_dec = arrange_arrivals(dec_messages, dec_extended, dec_width)
    grid_rows = grid_latent.shape[0]
    decoded = jax.ops.segment_sum(
        arrived_dec.astype(jnp.float32), dec_dst_rows.reshape(-1), num_segments=grid_rows
    )
    live_rows = jnp.arange(grid_rows, dtype=jnp.int32) < grid_count[0]
    grid_out = jnp.where(live_rows[:, None], grid_latent.astype(jnp.float32) + decoded, 0.0).astype(
        jnp.bfloat16
    )
    return (hidden_out, grid_out)


def solution(mesh):
    placed = (
        P(("ens", "seq"), ("mp", "sub")),
        P(("ens", "seq")),
        P(("ens", "seq"), ("mp", "sub")),
        P(("ens", "seq"), None, None),
        P(("ens", "seq"), None, None),
        P(("ens", "seq"), None, None),
        P(("ens", "seq"), None, None),
        P(("ens", "seq"), None, None),
        P(("ens", "seq"), None, None),
        P(),
        P(None, ("mp", "sub")),
        P(("mp", "sub"), None),
        P(None, ("mp", "sub")),
        P(("mp", "sub")),
        P(("mp", "sub"), None),
        P(),
    )
    return jax.shard_map(
        shards,
        mesh=mesh,
        in_specs=placed,
        out_specs=(P(("ens", "seq"), ("mp", "sub")), P(("ens", "seq"), ("mp", "sub"))),
        check_vma=False,
    )
```

profile of v0, /device:TPU:0, one launch (start us, length us, event | category | flops | bytes accessed | tf_op | source)
XLA Modules:
  0.0 323.1 jit_solution(15461693998175101110)
XLA Ops:
  8.9 17.2 %gather_fusion = bf16[4096,256]{1,0:T(8,128)(2,1)} fusion(bf16[2048,256]{1,0:T(8,128)(2,1)} %param.16, s32[4096]{0:T(1024)S(1)} %broadcast_clamp_fusion.1), kind=kCustom, calls=%fused_computation | custom fusion | bytes 4210688 | tf_op jit(solution)/shard_map/jit(_take)/gather | solution.py:48
  26.1 3.2 multiply_convert_fusion.1
  29.4 4.9 %collective-permute-start = (bf16[512,256]{1,0:T(8,128)(2,1)S(1)}, bf16[512,256]{1,0:T(8,128)(2,1)S(1)}, u32[]{:S(2)}, u32[]{:S(2)}) collective-permute-start(bf16[512,256]{1,0:T(8,128)(2,1)S(1)} %get-tuple-element.4), channel_id=1, source_target_pairs={{0,4},{4,8},{8,12},{1,5},{5,9},{9,13},{2,6},{6,10},{10,14},{3,7},{... | collective-permute-start | bytes 786440 | tf_op jit(solution)/shard_map/ppermute | solution.py:21
  36.9 2.9 collective-permute-done
  39.8 4.1 %collective-permute-done.1 = bf16[512,256]{1,0:T(8,128)(2,1)S(1)} collective-permute-done((bf16[512,256]{1,0:T(8,128)(2,1)S(1)}, bf16[512,256]{1,0:T(8,128)(2,1)S(1)}, u32[]{:S(2)}, u32[]{:S(2)}) %collective-permute-start.1) | collective-permute-done | bytes 262176 | tf_op jit(solution)/shard_map/ppermute | solution.py:23
  44.7 25.4 %scatter_custom_fusion = f32[1024,256]{1,0:T(8,128)S(1)} fusion(f32[1024,256]{1,0:T(8,128)S(1)} %convert_element_type.81, s32[4096]{0:T(1024)} %bitcast.75, bf16[3072,256]{1,0:T(8,128)(2,1)} %slice.117, bf16[]{:T(256)} %constant.130, bf16[512,256]{1,0:T(8,128)(2,1)} %copy-done.8, bf16[512,256]{1,0:T(8,128)(2,1)S(1)} %collective-permute-done), kind=kCustom, calls=%fused_computation.50 | custom fusion | flops 7340032 | bytes 3146240 | tf_op jit(solution)/shard_map/scatter-add | solution.py:83
  71.3 2.1 fusion.37
  73.3 21.0 %all-gather.2.cloned.1.call-done = bf16[1024,1024]{1,0:T(8,128)(2,1)} async-done(((bf16[1024,256]{1,0:T(8,128)(2,1)}), bf16[1024,1024]{1,0:T(8,128)(2,1)}) %all-gather.2.cloned.1.call-update) | async-done | bytes 2097168 | tf_op jit(solution)/shard_map/all_gather | solution.py:88
  94.3 2.1 convert_reduce_fusion
  96.4 2.3 fusion.16
  98.7 2.2 convolution_convert_fusion
  101.1 3.4 %collective-permute-start.2 = (bf16[512,2,256]{0,2,1:T(8,128)(2,1)S(1)}, bf16[512,2,256]{0,2,1:T(8,128)(2,1)S(1)}, u32[]{:S(2)}, u32[]{:S(2)}) collective-permute-start(bf16[512,2,256]{0,2,1:T(8,128)(2,1)S(1)} %bitcast.65), channel_id=1, source_target_pairs={{0,4},{4,8},{8,12},{1,5},{5,9},{9,13},{2,6},{6,10},{10,14},{3,7},{... | collective-permute-start | bytes 1572872 | tf_op jit(solution)/shard_map/ppermute | solution.py:21
  105.7 1.5 collective-permute-start.3
  107.2 8.9 %collective-permute-done.2 = bf16[512,2,256]{0,2,1:T(8,128)(2,1)S(1)} collective-permute-done((bf16[512,2,256]{0,2,1:T(8,128)(2,1)S(1)}, bf16[512,2,256]{0,2,1:T(8,128)(2,1)S(1)}, u32[]{:S(2)}, u32[]{:S(2)}) %collective-permute-start.2) | collective-permute-done | bytes 524320 | tf_op jit(solution)/shard_map/ppermute | solution.py:21
  116.1 6.3 %fusion.58 = f32[4,512,1536]{2,1,0:T(8,128)} fusion(bf16[1024,2,4,64]{0,3,2,1:T(8,128)(2,1)S(1)} %copy_bitcast_fusion, bf16[512,2,4,64]{0,3,2,1:T(8,128)(2,1)S(1)} %bitcast.60, bf16[1024,4,3,64]{0,3,2,1:T(8,128)(2,1)S(1)} %bitcast.58), kind=kOutput, calls=%fused_computation.91 | convolution fusion | flops 404226048 | bytes 14417920 | tf_op jit(solution)/shard_map/qhd,khd->hqk/dot_general | solution.py:108
  122.4 6.4 %fusion.54 = f32[4,512,1536]{2,1,0:T(8,128)} fusion(bf16[512,2,4,64]{0,3,2,1:T(8,128)(2,1)S(1)} %bitcast.62, bf16[1024,2,4,64]{0,3,2,1:T(8,128)(2,1)S(1)} %copy_bitcast_fusion, bf16[1024,4,3,64]{0,3,2,1:T(8,128)(2,1)S(1)} %bitcast.59), kind=kOutput, calls=%fused_computation.87 | convolution fusion | flops 404226048 | bytes 14417920 | tf_op jit(solution)/shard_map/qhd,khd->hqk/dot_general | solution.py:108
  128.8 16.5 %fusion.115 = (f32[4,512]{1,0:T(4,128)S(1)}, f32[4,512,1536]{2,1,0:T(8,128)}) fusion(f32[4,512,1536]{2,1,0:T(8,128)} %fusion.58, pred[512,1536]{1,0:T(8,128)(4,1)S(1)} %copy-done.5), kind=kOutput, calls=%fused_computation.163 | output fusion | flops 18875904 | bytes 25960448 | tf_op jit(solution)/shard_map/sub | solution.py:120
  145.3 6.7 %fusion.46 = bf16[4,64,512]{2,1,0:T(8,128)(2,1)S(1)} fusion(f32[4,512,1536]{2,1,0:T(8,128)} %get-tuple-element.11, f32[4,512]{1,0:T(4,128)S(1)} %get-tuple-element.10, bf16[512,2,4,64]{0,3,2,1:T(8,128)(2,1)S(1)} %bitcast.61, bf16[1024,2,4,64]{0,3,2,1:T(8,128)(2,1)S(1)} %copy_bitcast_fusion), kind=kOutput, calls=%fused_computation.78 | convolution fusion | flops 410648576 | bytes 14426112 | tf_op jit(solution)/shard_map/hqk,khd->qhd/dot_general | solution.py:122
  151.9 16.1 %fusion.114 = (f32[4,512]{1,0:T(4,128)S(1)}, f32[4,512,1536]{2,1,0:T(8,128)}) fusion(f32[4,512,1536]{2,1,0:T(8,128)} %fusion.54, pred[512,1536]{1,0:T(8,128)(4,1)S(1)} %fusion.39), kind=kOutput, calls=%fused_computation.162 | output fusion | flops 18875904 | bytes 25960448 | tf_op jit(solution)/shard_map/sub | solution.py:120
  168.0 6.7 %fusion.45 = bf16[4,64,512]{2,1,0:T(8,128)(2,1)S(1)} fusion(f32[4,512,1536]{2,1,0:T(8,128)} %get-tuple-element.9, f32[4,512]{1,0:T(4,128)S(1)} %get-tuple-element.8, bf16[1024,2,4,64]{0,3,2,1:T(8,128)(2,1)S(1)} %copy_bitcast_fusion, bf16[512,2,4,64]{0,3,2,1:T(8,128)(2,1)S(1)} %bitcast.63), kind=kOutput, calls=%fused_computation.77 | convolution fusion | flops 410648576 | bytes 14426112 | tf_op jit(solution)/shard_map/hqk,khd->qhd/dot_general | solution.py:122
  174.8 2.7 fusion.61
  177.5 16.8 %add_convert_fusion = bf16[1024,1024]{1,0:T(8,128)(2,1)} fusion(f32[1024,1024]{1,0:T(8,128)} %fusion.61, bf16[1024,1024]{1,0:T(8,128)(2,1)S(1)} %copy-done, f32[1024]{0:T(1024)S(1)} %get-tuple-element.16, bf16[1024,1024]{1,0:T(8,128)(2,1)} %param.28, f32[1024]{0:T(1024)S(1)} %get-tuple-element.17, bf16[1024,1024]{1,0:T(8,128)(2,1)} %all-gather.2.cloned.1.call-done, ...), kind=kOutput, calls=%fused_computation.36 | convolution fusion | flops 4372561920 | bytes 12603392 | tf_op jit(solution)/shard_map/dot_general | solution.py:134
  194.4 32.5 %reduce-scatter.2.cloned.1.call-done = bf16[1024,256]{1,0:T(8,128)(2,1)} async-done(((bf16[1024,1024]{1,0:T(8,128)(2,1)}), bf16[1024,256]{1,0:T(8,128)(2,1)}) %reduce-scatter.2.cloned.1.call-update) | async-done | bytes 524304 | tf_op jit(solution)/shard_map/reduce_scatter | solution.py:137
  226.9 1.5 add_convert_fusion.1
  228.5 25.0 %gather_fusion.1 = bf16[6144,256]{1,0:T(8,128)(2,1)} fusion(bf16[1024,256]{1,0:T(8,128)(2,1)S(1)} %add_convert_fusion.1, s32[6144]{0:T(1024)S(1)} %broadcast_clamp_fusion), kind=kCustom, calls=%fused_computation.1 | custom fusion | bytes 6316032 | tf_op jit(solution)/shard_map/jit(_take)/gather | solution.py:48
  253.4 4.7 %multiply_convert_fusion = bf16[6144,256]{1,0:T(8,128)(2,1)S(1)} fusion(f32[6144]{0:T(1024)S(1)} %bitcast.72, bf16[6144,256]{1,0:T(8,128)(2,1)} %gather_fusion.1, pred[6144]{0:T(1024)(128)(4,1)S(1)} %compare_and_fusion), kind=kLoop, calls=%fused_computation.16 | loop fusion | flops 6291456 | bytes 6322176 | tf_op jit(solution)/shard_map/convert_element_type | solution.py:51
  258.2 3.4 %collective-permute-start.4 = (bf16[512,256]{1,0:T(8,128)(2,1)S(1)}, bf16[512,256]{1,0:T(8,128)(2,1)S(1)}, u32[]{:S(2)}, u32[]{:S(2)}) collective-permute-start(bf16[512,256]{1,0:T(8,128)(2,1)S(1)} %get-tuple-element.2), channel_id=1, source_target_pairs={{0,4},{4,8},{8,12},{1,5},{5,9},{9,13},{2,6},{6,10},{10,14},{3,7},{... | collective-permute-start | bytes 786440 | tf_op jit(solution)/shard_map/ppermute | solution.py:21
  262.9 1.5 convert_element_type.103
  265.1 1.7 slice.129
  267.1 4.1 %collective-permute-done.5 = bf16[512,256]{1,0:T(8,128)(2,1)S(1)} collective-permute-done((bf16[512,256]{1,0:T(8,128)(2,1)S(1)}, bf16[512,256]{1,0:T(8,128)(2,1)S(1)}, u32[]{:S(2)}, u32[]{:S(2)}) %collective-permute-start.5) | collective-permute-done | bytes 262176 | tf_op jit(solution)/shard_map/ppermute | solution.py:23
  271.2 42.5 %scatter_custom_fusion.1 = f32[2048,256]{1,0:T(8,128)} fusion(f32[2048,256]{1,0:T(8,128)} %convert_element_type.103, s32[6144]{0:T(1024)} %bitcast.74, bf16[5120,256]{1,0:T(8,128)(2,1)} %slice.129, bf16[]{:T(256)} %constant.130, bf16[512,256]{1,0:T(8,128)(2,1)S(1)} %collective-permute-done.5, bf16[512,256]{1,0:T(8,128)(2,1)S(1)} %collective-permute-done.4), kind=kCustom, calls=%fused_computation.14 | custom fusion | flops 11010048 | bytes 5243392 | tf_op jit(solution)/shard_map/scatter-add | solution.py:146
  313.7 2.5 select_convert_fusion
  (64 shorter events, 9.2 us)
Async XLA Ops:
  7.2 170.3 %copy-start = (bf16[1024,1024]{1,0:T(8,128)(2,1)S(1)}, bf16[1024,1024]{1,0:T(8,128)(2,1)}, u32[]{:S(2)}) copy-start(bf16[1024,1024]{1,0:T(8,128)(2,1)} %param.30) | copy-start | bytes 6291460
  7.2 87.1 %all-gather.2.cloned.1.call-start = ((), (), s32[]{:S(2)}) async-start(), calls=%async_computation.1 | async-start | bytes 2621440 | tf_op jit(solution)/shard_map/all_gather | solution.py:88
  8.8 17.2 %copy-start.11 = (f32[1,32,128]{2,1,0:T(8,128)S(1)}, f32[1,32,128]{2,1,0:T(8,128)}, u32[]{:S(2)}) copy-start(f32[1,32,128]{2,1,0:T(8,128)} %param.21) | copy-start | bytes 49156
  26.1 10.8 %copy-start.6 = (bf16[1024,256]{1,0:T(8,128)(2,1)S(1)}, bf16[1024,256]{1,0:T(8,128)(2,1)}, u32[]{:S(2)}) copy-start(bf16[1024,256]{1,0:T(8,128)(2,1)} %param.18) | copy-start | bytes 1572868
  29.4 10.5 %collective-permute-start = (bf16[512,256]{1,0:T(8,128)(2,1)S(1)}, bf16[512,256]{1,0:T(8,128)(2,1)S(1)}, u32[]{:S(2)}, u32[]{:S(2)}) collective-permute-start(bf16[512,256]{1,0:T(8,128)(2,1)S(1)} %get-tuple-element.4), channel_id=1, source_target_pairs={{0,4},{4,8},{8,12},{1,5},{5,9},{9,13},{2,6},{6,10},{10,14},{3,7},{... | collective-permute-start | bytes 786440 | tf_op jit(solution)/shard_map/ppermute | solution.py:21
  34.3 9.7 %collective-permute-start.1 = (bf16[512,256]{1,0:T(8,128)(2,1)S(1)}, bf16[512,256]{1,0:T(8,128)(2,1)S(1)}, u32[]{:S(2)}, u32[]{:S(2)}) collective-permute-start(bf16[512,256]{1,0:T(8,128)(2,1)S(1)} %get-tuple-element.5), channel_id=1, source_target_pairs={{4,0},{8,4},{12,8},{5,1},{9,5},{13,9},{6,2},{10,6},{14,10},{7,3},{... | collective-permute-start | bytes 786440 | tf_op jit(solution)/shard_map/ppermute | solution.py:23
  36.9 34.4 %copy-start.12 = (s32[1024]{0:T(1024)S(1)}, s32[1024]{0:T(1024)}, u32[]{:S(2)}) copy-start(s32[1024]{0:T(1024)} %param.31) | copy-start | bytes 12292
  36.9 34.4 %copy-start.13 = (s32[1024]{0:T(1024)S(1)}, s32[1024]{0:T(1024)}, u32[]{:S(2)}) copy-start(s32[1024]{0:T(1024)} %param.29) | copy-start | bytes 12292
  44.0 0.7 copy-start.8
  70.1 30.8 %copy-start.3 = (f32[1024,256]{1,0:T(8,128)}, f32[1024,256]{1,0:T(8,128)S(1)}, u32[]{:S(2)}) copy-start(f32[1024,256]{1,0:T(8,128)S(1)} %scatter_custom_fusion) | copy-start | bytes 3145732
  70.1 28.6 %copy-start.15 = (f32[1024]{0:T(1024)S(1)}, f32[1024]{0:T(1024)}, u32[]{:S(2)}) copy-start(f32[1024]{0:T(1024)} %param.25) | copy-start | bytes 12292
  71.1 155.8 %reduce-scatter.2.cloned.1.call-start = ((), (), s32[]{:S(2)}) async-start(), calls=%async_computation.2 | async-start | bytes 2621440 | tf_op jit(solution)/shard_map/reduce_scatter | solution.py:137
  94.3 4.4 %copy-start.4 = (bf16[1024,1024]{1,0:T(8,128)(2,1)S(1)}, bf16[1024,1024]{1,0:T(8,128)(2,1)}, u32[]{:S(2)}) copy-start(bf16[1024,1024]{1,0:T(8,128)(2,1)} %all-gather.2.cloned.1.call-done) | copy-start | bytes 6291460
  94.3 4.4 %copy-start.14 = (bf16[1024,768]{1,0:T(8,128)(2,1)S(1)}, bf16[1024,768]{1,0:T(8,128)(2,1)}, u32[]{:S(2)}) copy-start(bf16[1024,768]{1,0:T(8,128)(2,1)} %param.26) | copy-start | bytes 4718596
  101.1 15.0 %collective-permute-start.2 = (bf16[512,2,256]{0,2,1:T(8,128)(2,1)S(1)}, bf16[512,2,256]{0,2,1:T(8,128)(2,1)S(1)}, u32[]{:S(2)}, u32[]{:S(2)}) collective-permute-start(bf16[512,2,256]{0,2,1:T(8,128)(2,1)S(1)} %bitcast.65), channel_id=1, source_target_pairs={{0,4},{4,8},{8,12},{1,5},{5,9},{9,13},{2,6},{6,10},{10,14},{3,7},{... | collective-permute-start | bytes 1572872 | tf_op jit(solution)/shard_map/ppermute | solution.py:21
  105.7 16.7 %collective-permute-start.3 = (bf16[512,2,256]{0,2,1:T(8,128)(2,1)S(1)}, bf16[512,2,256]{0,2,1:T(8,128)(2,1)S(1)}, u32[]{:S(2)}, u32[]{:S(2)}) collective-permute-start(bf16[512,2,256]{0,2,1:T(8,128)(2,1)S(1)} %bitcast.64), channel_id=1, source_target_pairs={{4,0},{8,4},{12,8},{5,1},{9,5},{13,9},{6,2},{10,6},{14,10},{7,3},{... | collective-permute-start | bytes 1572872 | tf_op jit(solution)/shard_map/ppermute | solution.py:23
  122.4 6.4 %copy-start.5 = (pred[512,1536]{1,0:T(8,128)(4,1)S(1)}, pred[512,1536]{1,0:T(8,128)(4,1)}, u32[]{:S(2)}) copy-start(pred[512,1536]{1,0:T(8,128)(4,1)} %fusion.37) | copy-start | bytes 2359300
  168.0 6.7 %copy-start.7 = (bf16[256,1024]{1,0:T(8,128)(2,1)S(1)}, bf16[256,1024]{1,0:T(8,128)(2,1)}, u32[]{:S(2)}) copy-start(bf16[256,1024]{1,0:T(8,128)(2,1)} %param.27) | copy-start | bytes 1572868
  177.5 16.9 %copy-start.9 = (s32[1,48,128]{2,1,0:T(8,128)S(1)}, s32[1,48,128]{2,1,0:T(8,128)}, u32[]{:S(2)}) copy-start(s32[1,48,128]{2,1,0:T(8,128)} %param.22) | copy-start | bytes 73732
  228.4 25.0 %copy-start.1 = (bf16[1024,256]{1,0:T(8,128)(2,1)}, bf16[1024,256]{1,0:T(8,128)(2,1)S(1)}, u32[]{:S(2)}) copy-start(bf16[1024,256]{1,0:T(8,128)(2,1)S(1)} %add_convert_fusion.1) | copy-start | bytes 1572868
  228.4 25.0 %copy-start.10 = (f32[1,48,128]{2,1,0:T(8,128)S(1)}, f32[1,48,128]{2,1,0:T(8,128)}, u32[]{:S(2)}) copy-start(f32[1,48,128]{2,1,0:T(8,128)} %param.24) | copy-start | bytes 73732
  253.4 9.5 %copy-start.2 = (bf16[2048,256]{1,0:T(8,128)(2,1)S(1)}, bf16[2048,256]{1,0:T(8,128)(2,1)}, u32[]{:S(2)}) copy-start(bf16[2048,256]{1,0:T(8,128)(2,1)} %param.16) | copy-start | bytes 3145732
  258.2 8.9 %collective-permute-start.4 = (bf16[512,256]{1,0:T(8,128)(2,1)S(1)}, bf16[512,256]{1,0:T(8,128)(2,1)S(1)}, u32[]{:S(2)}, u32[]{:S(2)}) collective-permute-start(bf16[512,256]{1,0:T(8,128)(2,1)S(1)} %get-tuple-element.2), channel_id=1, source_target_pairs={{0,4},{4,8},{8,12},{1,5},{5,9},{9,13},{2,6},{6,10},{10,14},{3,7},{... | collective-permute-start | bytes 786440 | tf_op jit(solution)/shard_map/ppermute | solution.py:21
  261.6 9.6 %collective-permute-start.5 = (bf16[512,256]{1,0:T(8,128)(2,1)S(1)}, bf16[512,256]{1,0:T(8,128)(2,1)S(1)}, u32[]{:S(2)}, u32[]{:S(2)}) collective-permute-start(bf16[512,256]{1,0:T(8,128)(2,1)S(1)} %get-tuple-element.3), channel_id=1, source_target_pairs={{4,0},{8,4},{12,8},{5,1},{9,5},{13,9},{6,2},{10,6},{14,10},{7,3},{... | collective-permute-start | bytes 786440 | tf_op jit(solution)/shard_map/ppermute | solution.py:23
Sparse Core Ops, SparseCore 0:
  71.2 23.0 all-gather.1
  194.5 32.4 reduce-scatter.1
where the time goes:
time: 324 us; the launch traced here: 323 us
  other arithmetic  124 us (38%)
  waiting for transfers between devices  74 us (23%)
  matrix products  47.8 us (15%)
  local copies, waits for them, and re-layouts  46.1 us (14%)
  starting transfers between devices  15.9 us (5%)
  between operations  15.1 us (5%)
    scatter-add x1, other arithmetic, shards(): jax.ops.segment_sum(arrived_dec.astype(jnp.float32), dec_dst_rows.reshape...  42.5 us
    gather x2, local copies, waits for them, and re-layouts, edge_messages(): jnp.take(source, src_rows.reshape(-1), axis=0).astype(jnp.float32)  42.2 us
    sub x2, other arithmetic, shards(): expo = jnp.exp(scores - peak)  32.6 us
    reduce_scatter x1, waiting for transfers between devices, shards(): lax.psum_scatter((attn_part + mlp_part).astype(jnp.bfloat16), ('mp', 'sub...  32.5 us
    scatter-add x1, other arithmetic, shards(): jax.ops.segment_sum(arrived.astype(jnp.float32), enc_dst_rows.reshape(-1)...  25.4 us
    all_gather x1, waiting for transfers between devices, shards(): full_rows = lax.all_gather(latent, ('mp', 'sub'), axis=1, tiled=True)  21 us
    dot_general x1, matrix products, shards(): jnp.dot(activated, w_down, preferred_element_type=jnp.float32)  16.8 us
    dot_general x2, matrix products, shards(): jnp.einsum('hqk,khd->qhd', attn_weights, value_block, preferred_element_t...  13.4 us
  transfers between devices with their start and end apart: 8, of which 7 were waited for; matrix products, arithmetic and copies ran while one was open for 4% of the time, Pallas kernels for 0%

commit v1 on v0

v1 whole, which is shorter than its diff:
```python
import functools

import jax
import jax.numpy as jnp
from jax import lax
from jax.experimental import pallas as pl
from jax.experimental.pallas import tpu as pltpu
from jax.sharding import PartitionSpec as P

HD = 64
WIN = 512
TILE = 128
ESIDE = 4
DSIDE = 4
GROUP = 8
BLOCK = 256
LIMIT = 60 * 1024 * 1024
VM = pl.BlockSpec(memory_space=pltpu.VMEM)
DMA = pltpu.SemaphoreType.DMA
MESH = pl.DeviceIdType.MESH


def turned(row):
    return jnp.broadcast_to(row, (TILE, TILE)).T


def gather_group(src, weight, table):
    rows, columns = table.shape
    lane = lax.broadcasted_iota(jnp.int32, (TILE, rows), 1).astype(jnp.int16)
    picks, scales = [], []
    for tile in range(src.shape[0]):
        col = turned(src[tile : tile + 1]).astype(jnp.int16)
        col = jnp.concatenate([col] * (rows // TILE), axis=1)
        picks.append(jnp.where(lane == col, jnp.bfloat16(1), jnp.bfloat16(0)))
        scale = turned(weight[tile : tile + 1])
        scales.append(jnp.concatenate([scale] * (columns // TILE), axis=1))
    picked = jnp.dot(jnp.concatenate(picks, axis=0), table, preferred_element_type=jnp.float32)
    return (picked * jnp.concatenate(scales, axis=0)).astype(jnp.bfloat16)


def scatter_group(dst, messages, rows, first=0):
    line = lax.broadcasted_iota(jnp.int32, (rows, TILE), 0).astype(jnp.int16)
    spots = []
    for tile in range(dst.shape[0]):
        row = jnp.broadcast_to(dst[tile : tile + 1] - first, (16, TILE)).astype(jnp.int16)
        row = jnp.concatenate([row] * (rows // 16), axis=0)
        spots.append(jnp.where(line == row, jnp.bfloat16(1), jnp.bfloat16(0)))
    return jnp.dot(jnp.concatenate(spots, axis=1), messages, preferred_element_type=jnp.float32)


def remote(src, dst, send, recv, **where):
    return pltpu.make_async_remote_copy(
        src_ref=src, dst_ref=dst, send_sem=send, recv_sem=recv, device_id=where, device_id_type=MESH
    )


def greet(peers):
    me, ends = lax.axis_index("seq"), lax.axis_size("seq") - 1
    barrier = pltpu.get_barrier_semaphore()
    for peer in peers:
        pl.semaphore_signal(barrier, inc=1, device_id=peer, device_id_type=MESH)

    @pl.when(me > 0)
    def _():
        pl.semaphore_signal(barrier, inc=1, device_id={"seq": me - 1}, device_id_type=MESH)

    @pl.when(me < ends)
    def _():
        pl.semaphore_signal(barrier, inc=1, device_id={"seq": me + 1}, device_id_type=MESH)

    near = jnp.where(me > 0, 1, 0) + jnp.where(me < ends, 1, 0)
    pl.semaphore_wait(barrier, near + len(peers))


def edge_sums(side, src_ref, weight_ref, dst_ref, table_ref, sums, sent, arrived, send, recv):
    me, ends = lax.axis_index("seq"), lax.axis_size("seq") - 1
    width = side * TILE
    rows = sums.shape[0]
    head, tail = pl.ds(0, width), pl.ds(width, width)
    to_left = remote(sent.at[head], arrived.at[tail], send.at[0], recv.at[0], seq=me - 1)
    to_right = remote(sent.at[tail], arrived.at[head], send.at[1], recv.at[1], seq=me + 1)
    sent[...] = gather_group(src_ref[: 2 * side], weight_ref[: 2 * side], table_ref[...])

    @pl.when(me > 0)
    def _():
        to_left.start()

    @pl.when(me < ends)
    def _():
        to_right.start()

    sums[...] = jnp.zeros_like(sums)

    @pl.loop(2 * side // GROUP, src_ref.shape[0] // GROUP)
    def _(step):
        here = pl.ds(pl.multiple_of(step * GROUP, GROUP), GROUP)
        messages = gather_group(src_ref[here, :], weight_ref[here, :], table_ref[...])
        sums[...] += scatter_group(dst_ref[here, :], messages, rows)

    @pl.when(me > 0)
    def _():
        to_right.wait_recv()

    @pl.when(me == 0)
    def _():
        arrived[head] = jnp.zeros((width, arrived.shape[1]), arrived.dtype)

    @pl.when(me < ends)
    def _():
        to_left.wait_recv()

    @pl.when(me == ends)
    def _():
        arrived[tail] = jnp.zeros((width, arrived.shape[1]), arrived.dtype)

    def finish():
        @pl.when(me > 0)
        def _():
            to_left.wait_send()

        @pl.when(me < ends)
        def _():
            to_right.wait_send()

    return finish


def layer_kernel(
    src_ref, weight_ref, dst_ref, grid_ref, embed_ref, gain_ref, up_exp_ref, down_exp_ref,
    qkv_hbm, up_hbm, down_hbm, out_hbm, hidden_ref,
    sums, sent, arrived, full, normed, queries, kv, mlp, parts, in1, out2, in2,
    w_qkv, w_up, w_down, w_out,
    w_sem, z_send, z_recv, ax_send, ax_recv, as_send, as_recv, kv_send, kv_recv,
    r1_send, r1_recv, r2_send, r2_recv,
):
    me, ends = lax.axis_index("seq"), lax.axis_size("seq") - 1
    mp, n_mp = lax.axis_index("mp"), lax.axis_size("mp")
    sub, n_sub = lax.axis_index("sub"), lax.axis_size("sub")
    rows, columns = embed_ref.shape
    blocks = n_mp * n_sub
    chunks = rows // BLOCK
    heads = queries.shape[1] // (2 * HD)
    own = mp * n_sub + sub

    loads = [
        pltpu.make_async_copy(src, dst, w_sem.at[i])
        for i, (src, dst) in enumerate(
            ((qkv_hbm, w_qkv), (up_hbm, w_up), (down_hbm, w_down), (out_hbm, w_out))
        )
    ]
    for load in loads:
        load.start()

    mp_at = lambda j: lax.rem(mp + j, n_mp)
    sub_at = lambda k: lax.rem(sub + k, n_sub)
    greet([{"mp": mp_at(j)} for j in range(1, n_mp)] + [{"sub": sub_at(k)} for k in range(1, n_sub)])

    def at_rows(chunk):
        return pl.ds(pl.multiple_of(chunk * BLOCK, BLOCK), BLOCK)

    def gather_mp(chunk, j, owner):
        piece = full.at[owner, at_rows(chunk)]
        return remote(piece, piece, ax_send.at[j - 1, chunk], ax_recv.at[j - 1, chunk], mp=mp_at(j))

    def gather_sub(chunk, k, j, owner):
        piece = full.at[owner, at_rows(chunk)]
        return remote(
            piece, piece, as_send.at[k - 1, j, chunk], as_recv.at[k - 1, j, chunk], sub=sub_at(k)
        )

    from_mp = lambda j: lax.rem(mp + n_mp - j, n_mp)
    from_sub = lambda k: lax.rem(sub + n_sub - k, n_sub)

    finish_edges = edge_sums(
        ESIDE, src_ref, weight_ref, dst_ref, grid_ref, sums, sent, arrived, z_send, z_recv
    )

    @pl.loop(0, chunks)
    def _(chunk):
        here = at_rows(chunk)
        total = scatter_group(dst_ref[: 2 * ESIDE], arrived[...], BLOCK, chunk * BLOCK)
        latent = embed_ref[here, :].astype(jnp.float32) + (sums[here, :] + total)
        full[own, here] = latent.astype(jnp.bfloat16)
        for j in range(1, n_mp):
            gather_mp(chunk, j, own).start()
        for k in range(1, n_sub):
            gather_sub(chunk, k, 0, own).start()

    def forward(chunk):
        for j in range(1, n_mp):
            owner = from_mp(j) * n_sub + sub
            gather_mp(chunk, j, owner).wait_recv()
            for k in range(1, n_sub):
                gather_sub(chunk, k, j, owner).start()

    def kv_copy(chunk, way):
        src = kv.at[pl.ds(pl.multiple_of(WIN + chunk * BLOCK, BLOCK), BLOCK)]
        shift = WIN + rows if way == 0 else WIN - rows
        dst = kv.at[pl.ds(pl.multiple_of(shift + chunk * BLOCK, BLOCK), BLOCK)]
        to = me - 1 if way == 0 else me + 1
        return remote(src, dst, kv_send.at[way, chunk], kv_recv.at[way, chunk], seq=to)

    to_left = range(WIN // BLOCK)
    to_right = range((rows - WIN) // BLOCK, chunks)

    def project(chunk):
        here = at_rows(chunk)
        for k in range(1, n_sub):
            for j in range(n_mp):
                owner = (from_mp(j) if j else mp) * n_sub + from_sub(k)
                gather_sub(chunk, k, j, owner).wait_recv()
        values = jnp.concatenate([full[t, here] for t in range(blocks)], axis=1).astype(jnp.float32)
        centered = values - jnp.mean(values, axis=-1, keepdims=True)
        row_var = jnp.mean(centered * centered, axis=-1, keepdims=True)
        rows_normed = (centered * lax.rsqrt(row_var + 1e-05) * gain_ref[...]).astype(jnp.bfloat16)
        normed[here, :] = rows_normed
        qkv = jnp.dot(rows_normed, w_qkv[...], preferred_element_type=jnp.float32)
        qkv = qkv.astype(jnp.bfloat16)
        blank = jnp.zeros((BLOCK, HD), jnp.bfloat16)
        inner = pl.ds(pl.multiple_of(WIN + chunk * BLOCK, BLOCK), BLOCK)
        for head in range(heads):
            at = head * 3 * HD
            wide = slice(head * 2 * HD, (head + 1) * 2 * HD)
            query = qkv[:, at : at + HD] * HD ** (-0.5)
            queries[here, wide] = jnp.concatenate([query, blank], axis=1)
            kv[inner, wide] = qkv[:, at + HD : at + 3 * HD]

        @pl.when((me > 0) & (chunk < to_left.stop))
        def _():
            kv_copy(chunk, 0).start()

        @pl.when((me < ends) & (chunk >= to_right.start))
        def _():
            kv_copy(chunk, 1).start()

    def feed_forward(chunk):
        here = at_rows(chunk)
        up = jnp.dot(normed[here, :], w_up[...], preferred_element_type=jnp.float32)
        up = up * jnp.exp2(up_exp_ref[...].astype(jnp.float32))
        active = (0.5 * up * (1.0 + lax.erf(up * 0.5**0.5))).astype(jnp.bfloat16)
        down = jnp.dot(active, w_down[...], preferred_element_type=jnp.float32)
        mlp[here, :] = down * jnp.exp2(down_exp_ref[...].astype(jnp.float32))

    edge_rows = jnp.zeros((WIN, kv.shape[1]), kv.dtype)

    @pl.when(me == 0)
    def _():
        kv[pl.ds(0, WIN)] = edge_rows

    @pl.when(me == ends)
    def _():
        kv[pl.ds(WIN + rows, WIN)] = edge_rows

    for load in loads:
        load.wait()
    forward(0)

    @pl.loop(0, chunks)
    def _(chunk):
        project(chunk)

        @pl.when(chunk + 1 < chunks)
        def _():
            forward(chunk + 1)

    @pl.loop(0, chunks)
    def _(chunk):
        feed_forward(chunk)

    @pl.when(me > 0)
    def _():
        for chunk in to_right:
            kv_copy(chunk, 1).wait_recv()

    @pl.when(me < ends)
    def _():
        for chunk in to_left:
            kv_copy(chunk, 0).wait_recv()

    def scatter_sub(chunk, k, m):
        return remote(
            parts.at[chunk, m * n_sub + sub_at(k)], in1.at[chunk, k - 1, m],
            r1_send.at[chunk, k - 1, m], r1_recv.at[chunk, k - 1, m], sub=sub_at(k),
        )

    def scatter_mp(chunk, j):
        return remote(
            out2.at[chunk, j - 1], in2.at[chunk, j - 1],
            r2_send.at[chunk, j - 1], r2_recv.at[chunk, j - 1], mp=mp_at(j),
        )

    pieces = (BLOCK + 2 * WIN) // BLOCK
    row = lax.broadcasted_iota(jnp.int32, (BLOCK, BLOCK), 0)
    lane = lax.broadcasted_iota(jnp.int32, (BLOCK, BLOCK), 1)
    front = lax.broadcasted_iota(jnp.int32, (BLOCK, 2 * HD), 1) < HD

    def attend(chunk):
        here = at_rows(chunk)
        outs = []
        for head in range(heads):
            wide = slice(head * 2 * HD, (head + 1) * 2 * HD)
            query = queries[here, wide]
            scored, windows = [], []
            for piece in range(pieces):
                at = pl.multiple_of(chunk * BLOCK + piece * BLOCK, BLOCK)
                window = kv[pl.ds(at, BLOCK), wide]
                windows.append(jnp.where(front, jnp.bfloat16(1), window))
                part = lax.dot_general(
                    query, window, (((1,), (1,)), ((), ())), preferred_element_type=jnp.float32
                )
                if piece * BLOCK != WIN:
                    spot = me * rows + at - WIN
                    inside = (spot >= 0) & (spot < (ends + 1) * rows)
                    part = part + jnp.where(inside, 0.0, -1e30)
                if piece == 0:
                    part = jnp.where(lane >= row, part, -1e30)
                if piece == pieces - 1:
                    part = jnp.where(lane <= row, part, -1e30)
                scored.append(part)
            scores = jnp.concatenate(scored, axis=1)
            peak = jnp.max(scores, axis=-1, keepdims=True)
            probs = jnp.exp(scores - peak).astype(jnp.bfloat16)
            mixed = jnp.dot(
                probs, jnp.concatenate(windows, axis=0), preferred_element_type=jnp.float32
            )
            rolled = pltpu.roll(mixed, HD, 1)
            outs.append(rolled / mixed if head % 2 == 0 else mixed / rolled)
        pairs = [jnp.where(front, outs[i], outs[i + 1]) for i in range(0, heads, 2)]
        attended = jnp.concatenate(pairs, axis=1).astype(jnp.bfloat16)
        out = jnp.dot(attended, w_out[...], preferred_element_type=jnp.float32) + mlp[here, :]
        out = out.astype(jnp.bfloat16)
        for t in range(blocks):
            parts[chunk, t] = out[:, t * columns : (t + 1) * columns]
        for k in range(1, n_sub):
            for m in range(n_mp):
                scatter_sub(chunk, k, m).start()

    def chip_sum(chunk, m):
        total = parts[chunk, m * n_sub + sub].astype(jnp.float32)
        for k in range(1, n_sub):
            total += in1[chunk, k - 1, m].astype(jnp.float32)
        return total

    def pass_on(chunk):
        for k in range(1, n_sub):
            for m in range(n_mp):
                scatter_sub(chunk, k, m).wait_recv()
        for j in range(1, n_mp):
            out2[chunk, j - 1] = chip_sum(chunk, mp_at(j)).astype(jnp.bfloat16)
            scatter_mp(chunk, j).start()

    @pl.loop(0, chunks)
    def _(chunk):
        attend(chunk)

        @pl.when(chunk > 0)
        def _():
            pass_on(chunk - 1)

    pass_on(chunks - 1)

    @pl.loop(0, chunks)
    def _(chunk):
        here = at_rows(chunk)
        total = chip_sum(chunk, mp)
        for j in range(1, n_mp):
            scatter_mp(chunk, j).wait_recv()
            total += in2[chunk, j - 1].astype(jnp.float32)
        hidden_ref[here, :] = (full[own, here].astype(jnp.float32) + total).astype(jnp.bfloat16)

    finish_edges()

    @pl.loop(0, chunks)
    def _(chunk):
        for j in range(1, n_mp):
            gather_mp(chunk, j, own).wait_send()
            scatter_mp(chunk, j).wait_send()
        for k in range(1, n_sub):
            for j in range(n_mp):
                gather_sub(chunk, k, j, own).wait_send()
                scatter_sub(chunk, k, j).wait_send()

    @pl.when(me > 0)
    def _():
        for chunk in to_left:
            kv_copy(chunk, 0).wait_send()

    @pl.when(me < ends)
    def _():
        for chunk in to_right:
            kv_copy(chunk, 1).wait_send()


def layer(src, weight, dst, grid, embed, gain, up_exp, down_exp, w_qkv, w_up, w_down, w_out):
    rows, columns = embed.shape
    n_mp, n_sub = lax.axis_size("mp"), lax.axis_size("sub")
    blocks, chunks = n_mp * n_sub, rows // BLOCK
    wide = w_qkv.shape[1] // (3 * HD) * 2 * HD
    half = lambda *shape: pltpu.VMEM(shape, jnp.bfloat16)
    full = lambda *shape: pltpu.VMEM(shape, jnp.float32)
    side = 2 * ESIDE * TILE
    return pl.pallas_call(
        layer_kernel,
        out_shape=jax.ShapeDtypeStruct((rows, columns), jnp.bfloat16),
        in_specs=[VM] * 8 + [pl.BlockSpec(memory_space=pl.ANY)] * 4,
        out_specs=VM,
        scratch_shapes=[
            full(rows, columns), half(side, columns), half(side, columns),
            half(blocks, rows, columns), half(rows, w_qkv.shape[0]),
            half(rows, wide), half(rows + 2 * WIN, wide), full(rows, w_down.shape[1]),
            half(chunks, blocks, BLOCK, columns), half(chunks, n_sub - 1, n_mp, BLOCK, columns),
            half(chunks, n_mp - 1, BLOCK, columns), half(chunks, n_mp - 1, BLOCK, columns),
            half(*w_qkv.shape), half(*w_up.shape), half(*w_down.shape), half(*w_out.shape),
            DMA((4,)), DMA((2,)), DMA((2,)),
            DMA((n_mp - 1, chunks)), DMA((n_mp - 1, chunks)),
            DMA((n_sub - 1, n_mp, chunks)), DMA((n_sub - 1, n_mp, chunks)),
            DMA((2, chunks)), DMA((2, chunks)),
            DMA((chunks, n_sub - 1, n_mp)), DMA((chunks, n_sub - 1, n_mp)),
            DMA((chunks, n_mp - 1)), DMA((chunks, n_mp - 1)),
        ],
        compiler_params=pltpu.CompilerParams(
            vmem_limit_bytes=LIMIT, collective_id=0, has_side_effects=True
        ),
        name="encode_layer",
    )(src, weight, dst, grid, embed, gain, up_exp, down_exp, w_qkv, w_up, w_down, w_out)


def decode_kernel(
    count_ref, src_ref, weight_ref, dst_ref, table_ref, base_ref, out_ref,
    sums, sent, arrived, z_send, z_recv,
):
    greet([])
    finish = edge_sums(
        DSIDE, src_ref, weight_ref, dst_ref, table_ref, sums, sent, arrived, z_send, z_recv
    )
    total = scatter_group(dst_ref[: 2 * DSIDE], arrived[...], out_ref.shape[0])
    total = base_ref[...].astype(jnp.float32) + (sums[...] + total)
    live = lax.broadcasted_iota(jnp.int32, total.shape, 0) < count_ref[0]
    out_ref[...] = jnp.where(live, total, 0.0).astype(out_ref.dtype)
    finish()


def decode(count, src, weight, dst, table, base):
    side = 2 * DSIDE * TILE
    columns = base.shape[1]
    return pl.pallas_call(
        decode_kernel,
        out_shape=jax.ShapeDtypeStruct(base.shape, base.dtype),
        in_specs=[pl.BlockSpec(memory_space=pltpu.SMEM)] + [VM] * 5,
        out_specs=VM,
        scratch_shapes=[
            pltpu.VMEM(base.shape, jnp.float32),
            pltpu.VMEM((side, columns), jnp.bfloat16),
            pltpu.VMEM((side, columns), jnp.bfloat16),
            DMA((2,)), DMA((2,)),
        ],
        compiler_params=pltpu.CompilerParams(
            vmem_limit_bytes=LIMIT, collective_id=1, has_side_effects=True
        ),
        name="decode",
    )(count, src, weight, dst, table, base)


def shards(
    grid_latent, grid_count, hidden_embed, enc_src_rows, enc_dst_rows, enc_weight,
    dec_src_rows, dec_dst_rows, dec_weight, norm_gain, w_qkv, w_out, w_up, up_exp, w_down, down_exp,
):
    hidden_out = layer(
        enc_src_rows[0], enc_weight[0], enc_dst_rows[0], grid_latent, hidden_embed,
        norm_gain[None, :], up_exp[None, :], down_exp[None, :], w_qkv, w_up, w_down, w_out,
    )
    grid_out = decode(
        grid_count, dec_src_rows[0], dec_weight[0], dec_dst_rows[0], hidden_out, grid_latent
    )
    return (hidden_out, grid_out)


def solution(mesh):
    rows = P(("ens", "seq"), ("mp", "sub"))
    tiles = P(("ens", "seq"), None, None)
    across, down = P(None, ("mp", "sub")), P(("mp", "sub"), None)
    placed = (
        rows, P(("ens", "seq")), rows, tiles, tiles, tiles, tiles, tiles, tiles,
        P(), across, down, across, P(("mp", "sub")), down, P(),
    )
    return jax.shard_map(shards, mesh=mesh, in_specs=placed, out_specs=(rows, rows), check_vma=False)
```

time: 324 us -> 85.2 us (0.26)
  other arithmetic: 124 us -> 0 us
  Pallas kernels: 0 us -> 80.7 us
  waiting for transfers between devices: 74 us -> 0 us
  matrix products: 47.8 us -> 0 us
  local copies, waits for them, and re-layouts: 46.1 us -> 3.06 us
  starting transfers between devices: 15.9 us -> 0 us
  between operations: 15.1 us -> 1.31 us
    pallas_call x0 -> x2, Pallas kernels: none -> 80.7 us  [the longest x1 55.1 us: layer(): pl.pallas_call(layer_kernel, out_shape=jax.ShapeDtypeStruct((rows, column...]
    scatter-add x2 -> x0, other arithmetic: 67.9 us -> none  [the longest x1 42.5 us: shards(): jax.ops.segment_sum(arrived_dec.astype(jnp.float32), dec_dst_rows.reshape...]
    dot_general x7 -> x0, matrix products: 47.8 us -> none  [the longest x1 16.8 us: shards(): jnp.dot(activated, w_down, preferred_element_type=jnp.float32)]
    gather x2 -> x0, local copies, waits for them, and re-layouts: 42.2 us -> none  [edge_messages(): jnp.take(source, src_rows.reshape(-1), axis=0).astype(jnp.float32)]
    sub x2 -> x0, other arithmetic: 32.6 us -> none  [shards(): expo = jnp.exp(scores - peak)]
    reduce_scatter x1 -> x0, waiting for transfers between devices: 32.5 us -> none  [shards(): lax.psum_scatter((attn_part + mlp_part).astype(jnp.bfloat16), ('mp', 'sub...]
    all_gather x1 -> x0, waiting for transfers between devices: 21 us -> none  [shards(): full_rows = lax.all_gather(latent, ('mp', 'sub'), axis=1, tiled=True)]
    ppermute x6 -> x0, waiting for transfers between devices: 20.5 us -> none  [the longest x3 12.2 us: padded(): lax.ppermute(tail, axis, [(i, (i + 1) % count) for i in range(ends)])]
  transfers between devices with their start and end apart: 8 -> 0, of which waited for: 7 -> 0; matrix products, arithmetic and copies ran while one was open for 4% -> 0% of each run, Pallas kernels for 0% -> 0%
where the time goes in v1:
time: 85.2 us; the launch traced here: 85 us
  Pallas kernels  80.7 us (95%)
  local copies, waits for them, and re-layouts  3.06 us (4%)
  between operations  1.31 us (2%)
    pallas_call x1, Pallas kernels, layer(): pl.pallas_call(layer_kernel, out_shape=jax.ShapeDtypeStruct((rows, column...  55.1 us
    pallas_call x1, Pallas kernels, decode(): pl.pallas_call(decode_kernel, out_shape=jax.ShapeDtypeStruct(base.shape,...  25.6 us
    unnamed x4, local copies, waits for them, and re-layouts  3.06 us

profile of v1, /device:TPU:0, one launch (start us, length us, event | category | flops | bytes accessed | tf_op | source)
XLA Modules:
  0.0 85.0 jit_solution(2252740308324981088)
XLA Ops:
  1.3 55.1 %encode_layer.1.table_ref = bf16[1024,256]{1,0:T(8,128)(2,1)} custom-call(s32[32,128]{1,0:T(8,128)} %bitcast.12, f32[32,128]{1,0:T(8,128)} %bitcast.13, s32[32,128]{1,0:T(8,128)} %bitcast.14, bf16[2048,256]{1,0:T(8,128)(2,1)} %base_ref.1, bf16[1024,256]{1,0:T(8,128)(2,1)} %embed_ref.1, f32[1,1024]{1,0:T(1,128)} %bitcast.15, s32[1,1024]{1,0:T(1,128)} %bitcast.16, ...), custom_call_target="tpu_custom_call" | custom-call | tf_op jit(solution)/shard_map/encode_layer/pallas_call | solution.py:402
  56.3 0.0 copy-start
  56.4 25.6 %decode.1 = bf16[2048,256]{1,0:T(8,128)(2,1)} custom-call(s32[1]{0:T(128)S(6)} %copy.20.count_ref, s32[48,128]{1,0:T(8,128)} %bitcast.9, f32[48,128]{1,0:T(8,128)} %bitcast.10, s32[48,128]{1,0:T(8,128)} %bitcast.11, bf16[1024,256]{1,0:T(8,128)(2,1)} %encode_layer.1.table_ref, bf16[2048,256]{1,0:T(8,128)(2,1)} %base_ref.1), custom_call_target="tpu_custom_call" | custom-call | tf_op jit(solution)/shard_map/decode/pallas_call | solution.py:446
  82.0 0.0 copy-done
  82.0 0.8 copy.21
  82.8 2.3 %copy.22 = bf16[2048,256]{1,0:T(8,128)(2,1)} copy(bf16[2048,256]{1,0:T(8,128)(2,1)} %decode.1) | data formatting | bytes 2097152
Async XLA Ops:
  56.3 25.6 %copy-start = (bf16[1024,256]{1,0:T(8,128)(2,1)S(1)}, bf16[1024,256]{1,0:T(8,128)(2,1)}, u32[]{:S(2)}) copy-start(bf16[1024,256]{1,0:T(8,128)(2,1)} %encode_layer.1.table_ref) | copy-start | bytes 1572868

commit v2 on v1

--- a/solution.py
+++ b/solution.py
@@ -72,14 +72,15 @@
     pl.semaphore_wait(barrier, near + len(peers))
 
 
-def edge_sums(side, src_ref, weight_ref, dst_ref, table_ref, sums, sent, arrived, send, recv):
+def edge_messages(side, src_ref, weight_ref, table_ref, sent, messages, send, recv, greeting=None):
     me, ends = lax.axis_index("seq"), lax.axis_size("seq") - 1
     width = side * TILE
-    rows = sums.shape[0]
     head, tail = pl.ds(0, width), pl.ds(width, width)
-    to_left = remote(sent.at[head], arrived.at[tail], send.at[0], recv.at[0], seq=me - 1)
-    to_right = remote(sent.at[tail], arrived.at[head], send.at[1], recv.at[1], seq=me + 1)
+    to_left = remote(sent.at[head], messages.at[tail], send.at[0], recv.at[0], seq=me - 1)
+    to_right = remote(sent.at[tail], messages.at[head], send.at[1], recv.at[1], seq=me + 1)
     sent[...] = gather_group(src_ref[: 2 * side], weight_ref[: 2 * side], table_ref[...])
+    if greeting is not None:
+        greet(greeting)
 
     @pl.when(me > 0)
     def _():
@@ -88,14 +89,12 @@
     @pl.when(me < ends)
     def _():
         to_right.start()
-
-    sums[...] = jnp.zeros_like(sums)
 
     @pl.loop(2 * side // GROUP, src_ref.shape[0] // GROUP)
     def _(step):
         here = pl.ds(pl.multiple_of(step * GROUP, GROUP), GROUP)
-        messages = gather_group(src_ref[here, :], weight_ref[here, :], table_ref[...])
-        sums[...] += scatter_group(dst_ref[here, :], messages, rows)
+        spots = pl.ds(pl.multiple_of(step * GROUP * TILE, GROUP * TILE), GROUP * TILE)
+        messages[spots, :] = gather_group(src_ref[here, :], weight_ref[here, :], table_ref[...])
 
     @pl.when(me > 0)
     def _():
@@ -103,7 +102,7 @@
 
     @pl.when(me == 0)
     def _():
-        arrived[head] = jnp.zeros((width, arrived.shape[1]), arrived.dtype)
+        messages[head] = jnp.zeros((width, messages.shape[1]), messages.dtype)
 
     @pl.when(me < ends)
     def _():
@@ -111,7 +110,7 @@
 
     @pl.when(me == ends)
     def _():
-        arrived[tail] = jnp.zeros((width, arrived.shape[1]), arrived.dtype)
+        messages[tail] = jnp.zeros((width, messages.shape[1]), messages.dtype)
 
     def finish():
         @pl.when(me > 0)
@@ -126,11 +125,12 @@
 
 
 def layer_kernel(
-    src_ref, weight_ref, dst_ref, grid_ref, embed_ref, gain_ref, up_exp_ref, down_exp_ref,
-    qkv_hbm, up_hbm, down_hbm, out_hbm, hidden_ref,
-    sums, sent, arrived, full, normed, queries, kv, mlp, parts, in1, out2, in2,
+    count_ref, src_ref, weight_ref, dst_ref, dec_src_ref, dec_weight_ref, dec_dst_ref,
+    grid_ref, embed_ref, gain_ref, up_exp_ref, down_exp_ref,
+    qkv_hbm, up_hbm, down_hbm, out_hbm, hidden_ref, result_ref,
+    sent, messages, dec_sent, dec_messages, full, normed, queries, kv, mlp, parts, in1, out2, in2,
     w_qkv, w_up, w_down, w_out,
-    w_sem, z_send, z_recv, ax_send, ax_recv, as_send, as_recv, kv_send, kv_recv,
+    w_sem, z_send, z_recv, d_send, d_recv, ax_send, ax_recv, as_send, as_recv, kv_send, kv_recv,
     r1_send, r1_recv, r2_send, r2_recv,
 ):
     me, ends = lax.axis_index("seq"), lax.axis_size("seq") - 1
@@ -153,7 +153,7 @@
 
     mp_at = lambda j: lax.rem(mp + j, n_mp)
     sub_at = lambda k: lax.rem(sub + k, n_sub)
-    greet([{"mp": mp_at(j)} for j in range(1, n_mp)] + [{"sub": sub_at(k)} for k in range(1, n_sub)])
+    peers = [{"mp": mp_at(j)} for j in range(1, n_mp)] + [{"sub": sub_at(k)} for k in range(1, n_sub)]
 
     def at_rows(chunk):
         return pl.ds(pl.multiple_of(chunk * BLOCK, BLOCK), BLOCK)
@@ -171,15 +171,19 @@
     from_mp = lambda j: lax.rem(mp + n_mp - j, n_mp)
     from_sub = lambda k: lax.rem(sub + n_sub - k, n_sub)
 
-    finish_edges = edge_sums(
-        ESIDE, src_ref, weight_ref, dst_ref, grid_ref, sums, sent, arrived, z_send, z_recv
+    finish_edges = edge_messages(
+        ESIDE, src_ref, weight_ref, grid_ref, sent, messages, z_send, z_recv, peers
     )
 
+    def turn(step):
+        return step % 2 * (chunks // 2) + step // 2 if chunks % 2 == 0 else step
+
     @pl.loop(0, chunks)
-    def _(chunk):
+    def _(step):
+        chunk = turn(step)
         here = at_rows(chunk)
-        total = scatter_group(dst_ref[: 2 * ESIDE], arrived[...], BLOCK, chunk * BLOCK)
-        latent = embed_ref[here, :].astype(jnp.float32) + (sums[here, :] + total)
+        total = scatter_group(dst_ref[...], messages[...], BLOCK, chunk * BLOCK)
+        latent = embed_ref[here, :].astype(jnp.float32) + total
         full[own, here] = latent.astype(jnp.bfloat16)
         for j in range(1, n_mp):
             gather_mp(chunk, j, own).start()
@@ -235,9 +239,21 @@
 
     def feed_forward(chunk):
         here = at_rows(chunk)
-        up = jnp.dot(normed[here, :], w_up[...], preferred_element_type=jnp.float32)
-        up = up * jnp.exp2(up_exp_ref[...].astype(jnp.float32))
-        active = (0.5 * up * (1.0 + lax.erf(up * 0.5**0.5))).astype(jnp.bfloat16)
+        rows_normed = normed[here, :]
+        units = w_up.shape[1]
+        width = min(256, units)
+
+        def rise(at):
+            return jnp.dot(
+                rows_normed, w_up[:, at : at + width], preferred_element_type=jnp.float32
+            )
+
+        later, pieces = rise(0), []
+        for at in range(0, units, width):
+            up, later = later, rise(at + width) if at + width < units else None
+            up = up * jnp.exp2(up_exp_ref[:, at : at + width].astype(jnp.float32))
+            pieces.append((0.5 * up * (1.0 + lax.erf(up * 0.5**0.5))).astype(jnp.bfloat16))
+        active = jnp.concatenate(pieces, axis=1)
         down = jnp.dot(active, w_down[...], preferred_element_type=jnp.float32)
         mlp[here, :] = down * jnp.exp2(down_exp_ref[...].astype(jnp.float32))
 
@@ -253,19 +269,23 @@
 
     for load in loads:
         load.wait()
-    forward(0)
-
-    @pl.loop(0, chunks)
-    def _(chunk):
-        project(chunk)
-
-        @pl.when(chunk + 1 < chunks)
+    forward(turn(0))
+    project(turn(0))
+    if chunks > 1:
+        forward(turn(1))
+    feed_forward(turn(0))
+
+    @pl.loop(1, chunks)
+    def _(step):
+        project(turn(step))
+
+        @pl.when(step + 1 < chunks)
         def _():
-            forward(chunk + 1)
-
-    @pl.loop(0, chunks)
-    def _(chunk):
-        feed_forward(chunk)
+            forward(turn(step + 1))
+
+    @pl.loop(1, chunks)
+    def _(step):
+        feed_forward(turn(step))
 
     @pl.when(me > 0)
     def _():
@@ -296,8 +316,8 @@
 
     def attend(chunk):
         here = at_rows(chunk)
-        outs = []
-        for head in range(heads):
+
+        def score(head):
             wide = slice(head * 2 * HD, (head + 1) * 2 * HD)
             query = queries[here, wide]
             scored, windows = [], []
@@ -317,12 +337,14 @@
                 if piece == pieces - 1:
                     part = jnp.where(lane <= row, part, -1e30)
                 scored.append(part)
-            scores = jnp.concatenate(scored, axis=1)
+            return jnp.concatenate(scored, axis=1), jnp.concatenate(windows, axis=0)
+
+        later, outs = score(0), []
+        for head in range(heads):
+            (scores, window), later = later, score(head + 1) if head + 1 < heads else None
             peak = jnp.max(scores, axis=-1, keepdims=True)
             probs = jnp.exp(scores - peak).astype(jnp.bfloat16)
-            mixed = jnp.dot(
-                probs, jnp.concatenate(windows, axis=0), preferred_element_type=jnp.float32
-            )
+            mixed = jnp.dot(probs, window, preferred_element_type=jnp.float32)
             rolled = pltpu.roll(mixed, HD, 1)
             outs.append(rolled / mixed if head % 2 == 0 else mixed / rolled)
         pairs = [jnp.where(front, outs[i], outs[i + 1]) for i in range(0, heads, 2)]
@@ -368,7 +390,22 @@
             total += in2[chunk, j - 1].astype(jnp.float32)
         hidden_ref[here, :] = (full[own, here].astype(jnp.float32) + total).astype(jnp.bfloat16)
 
+    finish_decoder = edge_messages(
+        DSIDE, dec_src_ref, dec_weight_ref, hidden_ref, dec_sent, dec_messages, d_send, d_recv
+    )
+    wider = 2 * BLOCK
+
+    @pl.loop(0, result_ref.shape[0] // wider)
+    def _(step):
+        first = pl.multiple_of(step * wider, wider)
+        here = pl.ds(first, wider)
+        total = scatter_group(dec_dst_ref[...], dec_messages[...], wider, first)
+        total = grid_ref[here, :].astype(jnp.float32) + total
+        live = lax.broadcasted_iota(jnp.int32, total.shape, 0) + first < count_ref[0]
+        result_ref[here, :] = jnp.where(live, total, 0.0).astype(jnp.bfloat16)
+
     finish_edges()
+    finish_decoder()
 
     @pl.loop(0, chunks)
     def _(chunk):
@@ -391,27 +428,34 @@
             kv_copy(chunk, 1).wait_send()
 
 
-def layer(src, weight, dst, grid, embed, gain, up_exp, down_exp, w_qkv, w_up, w_down, w_out):
+def layer(
+    count, src, weight, dst, dec_src, dec_weight, dec_dst,
+    grid, embed, gain, up_exp, down_exp, w_qkv, w_up, w_down, w_out,
+):
     rows, columns = embed.shape
     n_mp, n_sub = lax.axis_size("mp"), lax.axis_size("sub")
     blocks, chunks = n_mp * n_sub, rows // BLOCK
     wide = w_qkv.shape[1] // (3 * HD) * 2 * HD
     half = lambda *shape: pltpu.VMEM(shape, jnp.bfloat16)
     full = lambda *shape: pltpu.VMEM(shape, jnp.float32)
-    side = 2 * ESIDE * TILE
     return pl.pallas_call(
         layer_kernel,
-        out_shape=jax.ShapeDtypeStruct((rows, columns), jnp.bfloat16),
-        in_specs=[VM] * 8 + [pl.BlockSpec(memory_space=pl.ANY)] * 4,
-        out_specs=VM,
+        out_shape=(
+            jax.ShapeDtypeStruct((rows, columns), jnp.bfloat16),
+            jax.ShapeDtypeStruct(grid.shape, jnp.bfloat16),
+        ),
+        in_specs=[pl.BlockSpec(memory_space=pltpu.SMEM)] + [VM] * 11
+        + [pl.BlockSpec(memory_space=pl.ANY)] * 4,
+        out_specs=(VM, VM),
         scratch_shapes=[
-            full(rows, columns), half(side, columns), half(side, columns),
+            half(2 * ESIDE * TILE, columns), half(src.size, columns),
+            half(2 * DSIDE * TILE, columns), half(dec_src.size, columns),
             half(blocks, rows, columns), half(rows, w_qkv.shape[0]),
             half(rows, wide), half(rows + 2 * WIN, wide), full(rows, w_down.shape[1]),
             half(chunks, blocks, BLOCK, columns), half(chunks, n_sub - 1, n_mp, BLOCK, columns),
             half(chunks, n_mp - 1, BLOCK, columns), half(chunks, n_mp - 1, BLOCK, columns),
             half(*w_qkv.shape), half(*w_up.shape), half(*w_down.shape), half(*w_out.shape),
-            DMA((4,)), DMA((2,)), DMA((2,)),
+            DMA((4,)), DMA((2,)), DMA((2,)), DMA((2,)), DMA((2,)),
             DMA((n_mp - 1, chunks)), DMA((n_mp - 1, chunks)),
             DMA((n_sub - 1, n_mp, chunks)), DMA((n_sub - 1, n_mp, chunks)),
             DMA((2, chunks)), DMA((2, chunks)),
@@ -421,58 +465,53 @@
         compiler_params=pltpu.CompilerParams(
             vmem_limit_bytes=LIMIT, collective_id=0, has_side_effects=True
         ),
-        name="encode_layer",
-    )(src, weight, dst, grid, embed, gain, up_exp, down_exp, w_qkv, w_up, w_down, w_out)
-
-
-def decode_kernel(
-    count_ref, src_ref, weight_ref, dst_ref, table_ref, base_ref, out_ref,
-    sums, sent, arrived, z_send, z_recv,
-):
-    greet([])
-    finish = edge_sums(
-        DSIDE, src_ref, weight_ref, dst_ref, table_ref, sums, sent, arrived, z_send, z_recv
+        name="encode_layer_decode",
+    )(
+        count, src, weight, dst, dec_src, dec_weight, dec_dst,
+        grid, embed, gain, up_exp, down_exp, w_qkv, w_up, w_down, w_out,
     )
-    total = scatter_group(dst_ref[: 2 * DSIDE], arrived[...], out_ref.shape[0])
-    total = base_ref[...].astype(jnp.float32) + (sums[...] + total)
-    live = lax.broadcasted_iota(jnp.int32, total.shape, 0) < count_ref[0]
-    out_ref[...] = jnp.where(live, total, 0.0).astype(out_ref.dtype)
-    finish()
-
-
-def decode(count, src, weight, dst, table, base):
-    side = 2 * DSIDE * TILE
-    columns = base.shape[1]
+
+
+def hand_on_kernel(*refs):
+    count = (len(refs) - 1) // 2
+    sems = refs[-1]
+    copies = []
+    for i in range(count):
+        half = refs[i].shape[0] // 2
+        for j in range(2):
+            here = pl.ds(j * half, half)
+            copies.append(
+                pltpu.make_async_copy(refs[i].at[here], refs[count + i].at[here], sems.at[2 * i + j])
+            )
+    for copy in copies:
+        copy.start()
+    for copy in copies:
+        copy.wait()
+
+
+def hand_on(*arrays):
+    places = [pl.BlockSpec(memory_space=pl.ANY)] * len(arrays)
     return pl.pallas_call(
-        decode_kernel,
-        out_shape=jax.ShapeDtypeStruct(base.shape, base.dtype),
-        in_specs=[pl.BlockSpec(memory_space=pltpu.SMEM)] + [VM] * 5,
-        out_specs=VM,
-        scratch_shapes=[
-            pltpu.VMEM(base.shape, jnp.float32),
-            pltpu.VMEM((side, columns), jnp.bfloat16),
-            pltpu.VMEM((side, columns), jnp.bfloat16),
-            DMA((2,)), DMA((2,)),
-        ],
-        compiler_params=pltpu.CompilerParams(
-            vmem_limit_bytes=LIMIT, collective_id=1, has_side_effects=True
-        ),
-        name="decode",
-    )(count, src, weight, dst, table, base)
+        hand_on_kernel,
+        out_shape=tuple(jax.ShapeDtypeStruct(array.shape, array.dtype) for array in arrays),
+        in_specs=places,
+        out_specs=tuple(places),
+        scratch_shapes=[DMA((2 * len(arrays),))],
+        compiler_params=pltpu.CompilerParams(vmem_limit_bytes=LIMIT),
+        name="hand_on",
+    )(*arrays)
 
 
 def shards(
     grid_latent, grid_count, hidden_embed, enc_src_rows, enc_dst_rows, enc_weight,
     dec_src_rows, dec_dst_rows, dec_weight, norm_gain, w_qkv, w_out, w_up, up_exp, w_down, down_exp,
 ):
-    hidden_out = layer(
-        enc_src_rows[0], enc_weight[0], enc_dst_rows[0], grid_latent, hidden_embed,
+    hidden_out, grid_out = layer(
+        grid_count, enc_src_rows[0], enc_weight[0], enc_dst_rows[0],
+        dec_src_rows[0], dec_weight[0], dec_dst_rows[0], grid_latent, hidden_embed,
         norm_gain[None, :], up_exp[None, :], down_exp[None, :], w_qkv, w_up, w_down, w_out,
     )
-    grid_out = decode(
-        grid_count, dec_src_rows[0], dec_weight[0], dec_dst_rows[0], hidden_out, grid_latent
-    )
-    return (hidden_out, grid_out)
+    return hand_on(hidden_out, grid_out)
 
 
 def solution(mesh):

time: 85.2 us -> 122 us (1.43)
  Pallas kernels: 80.7 us -> 120 us
  local copies, waits for them, and re-layouts: 3.06 us -> 0 us
    pallas_call x2, Pallas kernels: 80.7 us -> 120 us  [the longest x1 71.5 us: layer(): pl.pallas_call(layer_kernel, out_shape=(jax.ShapeDtypeStruct((rows, colum...]
    unnamed x4 -> x0, local copies, waits for them, and re-layouts: 3.06 us -> none
where the time goes in v2:
time: 122 us
  Pallas kernels  120 us (98%)
  between operations  1.29 us (1%)
    pallas_call x1, Pallas kernels, layer(): pl.pallas_call(layer_kernel, out_shape=(jax.ShapeDtypeStruct((rows, colum...  71.5 us
    pallas_call x1, Pallas kernels, hand_on(): pl.pallas_call(hand_on_kernel, out_shape=tuple((jax.ShapeDtypeStruct(arra...  48.8 us

profile of v2, /device:TPU:0, one launch (start us, length us, event | category | flops | bytes accessed | tf_op | source)
XLA Modules:
  0.0 121.5 jit_solution(3571065352815931858)
XLA Ops:
  1.3 71.5 %encode_layer_decode.1 = (bf16[1024,256]{1,0:T(8,128)(2,1)}, bf16[2048,256]{1,0:T(8,128)(2,1)}) custom-call(s32[1]{0:T(128)S(6)} %copy.18.count_ref, s32[32,128]{1,0:T(8,128)} %bitcast.12, f32[32,128]{1,0:T(8,128)} %bitcast.13, s32[32,128]{1,0:T(8,128)} %bitcast.14, s32[48,128]{1,0:T(8,128)} %bitcast.9, f32[48,128]{1,0:T(8,128)} %bitcast.10, ...), custom_call_target="tpu_custom_call" | custom-call | tf_op jit(solution)/shard_map/encode_layer_decode/pallas_call | solution.py:441
  72.8 48.8 %hand_on.1 = (bf16[1024,256]{1,0:T(8,128)(2,1)}, bf16[2048,256]{1,0:T(8,128)(2,1)}) custom-call(bf16[1024,256]{1,0:T(8,128)(2,1)} %get-tuple-element.4.refs_0_, bf16[2048,256]{1,0:T(8,128)(2,1)} %get-tuple-element.5.refs_1_), custom_call_target="tpu_custom_call" | custom-call | tf_op jit(solution)/shard_map/hand_on/pallas_call | solution.py:494

commit v3 on v2

--- a/solution.py
+++ b/solution.py
@@ -24,12 +24,12 @@
     return jnp.broadcast_to(row, (TILE, TILE)).T
 
 
-def gather_group(src, weight, table):
+def gather_group(src, weight, table, first=0):
     rows, columns = table.shape
     lane = lax.broadcasted_iota(jnp.int32, (TILE, rows), 1).astype(jnp.int16)
     picks, scales = [], []
     for tile in range(src.shape[0]):
-        col = turned(src[tile : tile + 1]).astype(jnp.int16)
+        col = turned(src[tile : tile + 1] - first).astype(jnp.int16)
         col = jnp.concatenate([col] * (rows // TILE), axis=1)
         picks.append(jnp.where(lane == col, jnp.bfloat16(1), jnp.bfloat16(0)))
         scale = turned(weight[tile : tile + 1])
@@ -72,63 +72,91 @@
     pl.semaphore_wait(barrier, near + len(peers))
 
 
-def edge_messages(side, src_ref, weight_ref, table_ref, sent, messages, send, recv, greeting=None):
-    me, ends = lax.axis_index("seq"), lax.axis_size("seq") - 1
-    width = side * TILE
-    head, tail = pl.ds(0, width), pl.ds(width, width)
+def side_copies(side, sent, messages, send, recv):
+    me = lax.axis_index("seq")
+    head, tail = pl.ds(0, side * TILE), pl.ds(side * TILE, side * TILE)
     to_left = remote(sent.at[head], messages.at[tail], send.at[0], recv.at[0], seq=me - 1)
     to_right = remote(sent.at[tail], messages.at[head], send.at[1], recv.at[1], seq=me + 1)
-    sent[...] = gather_group(src_ref[: 2 * side], weight_ref[: 2 * side], table_ref[...])
-    if greeting is not None:
-        greet(greeting)
+    return to_left, to_right
+
+
+def start_sides(copies):
+    me, ends = lax.axis_index("seq"), lax.axis_size("seq") - 1
 
     @pl.when(me > 0)
     def _():
-        to_left.start()
+        copies[0].start()
 
     @pl.when(me < ends)
     def _():
-        to_right.start()
-
+        copies[1].start()
+
+
+def wait_sides(side, copies, messages):
+    me, ends = lax.axis_index("seq"), lax.axis_size("seq") - 1
+    blank = jnp.zeros((side * TILE, messages.shape[1]), messages.dtype)
+
+    @pl.when(me > 0)
+    def _():
+        copies[1].wait_recv()
+
+    @pl.when(me == 0)
+    def _():
+        messages[pl.ds(0, side * TILE)] = blank
+
+    @pl.when(me < ends)
+    def _():
+        copies[0].wait_recv()
+
+    @pl.when(me == ends)
+    def _():
+        messages[pl.ds(side * TILE, side * TILE)] = blank
+
+
+def finish_sides(copies):
+    me, ends = lax.axis_index("seq"), lax.axis_size("seq") - 1
+
+    @pl.when(me > 0)
+    def _():
+        copies[0].wait_send()
+
+    @pl.when(me < ends)
+    def _():
+        copies[1].wait_send()
+
+
+def side_messages(side, src_ref, weight_ref, table, sent, first=0, add=False):
+    found = gather_group(src_ref[: 2 * side], weight_ref[: 2 * side], table, first)
+    sent[...] = sent[...] + found if add else found
+
+
+def local_messages(side, src_ref, weight_ref, table_ref, messages, first=0, add=False):
     @pl.loop(2 * side // GROUP, src_ref.shape[0] // GROUP)
     def _(step):
         here = pl.ds(pl.multiple_of(step * GROUP, GROUP), GROUP)
         spots = pl.ds(pl.multiple_of(step * GROUP * TILE, GROUP * TILE), GROUP * TILE)
-        messages[spots, :] = gather_group(src_ref[here, :], weight_ref[here, :], table_ref[...])
-
-    @pl.when(me > 0)
-    def _():
-        to_right.wait_recv()
-
-    @pl.when(me == 0)
-    def _():
-        messages[head] = jnp.zeros((width, messages.shape[1]), messages.dtype)
-
-    @pl.when(me < ends)
-    def _():
-        to_left.wait_recv()
-
-    @pl.when(me == ends)
-    def _():
-        messages[tail] = jnp.zeros((width, messages.shape[1]), messages.dtype)
-
-    def finish():
-        @pl.when(me > 0)
-        def _():
-            to_left.wait_send()
-
-        @pl.when(me < ends)
-        def _():
-            to_right.wait_send()
-
-    return finish
+        found = gather_group(src_ref[here, :], weight_ref[here, :], table_ref[...], first)
+        messages[spots, :] = messages[spots, :] + found if add else found
+
+
+def local_sums(side, dst_ref, messages, sums, block):
+    @pl.loop(0, sums.shape[0] // block)
+    def _(step):
+        first = pl.multiple_of(step * block, block)
+        sums[pl.ds(first, block), :] = scatter_group(
+            dst_ref[2 * side :], messages[2 * side * TILE :], block, first
+        )
+
+
+def arrived_sums(side, dst_ref, messages, block, first):
+    return scatter_group(dst_ref[: 2 * side], messages[: 2 * side * TILE], block, first)
 
 
 def layer_kernel(
     count_ref, src_ref, weight_ref, dst_ref, dec_src_ref, dec_weight_ref, dec_dst_ref,
     grid_ref, embed_ref, gain_ref, up_exp_ref, down_exp_ref,
     qkv_hbm, up_hbm, down_hbm, out_hbm, hidden_ref, result_ref,
-    sent, messages, dec_sent, dec_messages, full, normed, queries, kv, mlp, parts, in1, out2, in2,
+    sums, sent, messages, dec_sent, dec_messages, full, normed, queries, kv, mlp, parts, in1, out2, in2,
     w_qkv, w_up, w_down, w_out,
     w_sem, z_send, z_recv, d_send, d_recv, ax_send, ax_recv, as_send, as_recv, kv_send, kv_recv,
     r1_send, r1_recv, r2_send, r2_recv,
@@ -171,9 +199,13 @@
     from_mp = lambda j: lax.rem(mp + n_mp - j, n_mp)
     from_sub = lambda k: lax.rem(sub + n_sub - k, n_sub)
 
-    finish_edges = edge_messages(
-        ESIDE, src_ref, weight_ref, grid_ref, sent, messages, z_send, z_recv, peers
-    )
+    encoder_copies = side_copies(ESIDE, sent, messages, z_send, z_recv)
+    side_messages(ESIDE, src_ref, weight_ref, grid_ref[...], sent)
+    greet(peers)
+    start_sides(encoder_copies)
+    local_messages(ESIDE, src_ref, weight_ref, grid_ref, messages)
+    local_sums(ESIDE, dst_ref, messages, sums.at[pl.ds(0, rows)], 2 * BLOCK)
+    wait_sides(ESIDE, encoder_copies, messages)
 
     def turn(step):
         return step % 2 * (chunks // 2) + step // 2 if chunks % 2 == 0 else step
@@ -182,7 +214,7 @@
     def _(step):
         chunk = turn(step)
         here = at_rows(chunk)
-        total = scatter_group(dst_ref[...], messages[...], BLOCK, chunk * BLOCK)
+        total = sums[here, :] + arrived_sums(ESIDE, dst_ref, messages, BLOCK, chunk * BLOCK)
         latent = embed_ref[here, :].astype(jnp.float32) + total
         full[own, here] = latent.astype(jnp.bfloat16)
         for j in range(1, n_mp):
@@ -381,8 +413,7 @@
 
     pass_on(chunks - 1)
 
-    @pl.loop(0, chunks)
-    def _(chunk):
+    def finish_rows(chunk):
         here = at_rows(chunk)
         total = chip_sum(chunk, mp)
         for j in range(1, n_mp):
@@ -390,22 +421,37 @@
             total += in2[chunk, j - 1].astype(jnp.float32)
         hidden_ref[here, :] = (full[own, here].astype(jnp.float32) + total).astype(jnp.bfloat16)
 
-    finish_decoder = edge_messages(
-        DSIDE, dec_src_ref, dec_weight_ref, hidden_ref, dec_sent, dec_messages, d_send, d_recv
-    )
+    early = rows - BLOCK
+    if early:
+        @pl.loop(0, chunks - 1)
+        def _(chunk):
+            finish_rows(chunk)
+
+        first_rows = hidden_ref.at[pl.ds(0, early)]
+        side_messages(DSIDE, dec_src_ref, dec_weight_ref, first_rows[...], dec_sent)
+        local_messages(DSIDE, dec_src_ref, dec_weight_ref, first_rows, dec_messages)
+    finish_rows(chunks - 1)
+    last_rows = hidden_ref.at[pl.ds(early, BLOCK)]
+    more = early > 0
+    decoder_copies = side_copies(DSIDE, dec_sent, dec_messages, d_send, d_recv)
+    side_messages(DSIDE, dec_src_ref, dec_weight_ref, last_rows[...], dec_sent, early, more)
+    start_sides(decoder_copies)
+    local_messages(DSIDE, dec_src_ref, dec_weight_ref, last_rows, dec_messages, early, more)
     wider = 2 * BLOCK
+    local_sums(DSIDE, dec_dst_ref, dec_messages, sums, wider)
+    wait_sides(DSIDE, decoder_copies, dec_messages)
 
     @pl.loop(0, result_ref.shape[0] // wider)
     def _(step):
         first = pl.multiple_of(step * wider, wider)
         here = pl.ds(first, wider)
-        total = scatter_group(dec_dst_ref[...], dec_messages[...], wider, first)
+        total = sums[here, :] + arrived_sums(DSIDE, dec_dst_ref, dec_messages, wider, first)
         total = grid_ref[here, :].astype(jnp.float32) + total
         live = lax.broadcasted_iota(jnp.int32, total.shape, 0) + first < count_ref[0]
         result_ref[here, :] = jnp.where(live, total, 0.0).astype(jnp.bfloat16)
 
-    finish_edges()
-    finish_decoder()
+    finish_sides(encoder_copies)
+    finish_sides(decoder_copies)
 
     @pl.loop(0, chunks)
     def _(chunk):
@@ -448,6 +494,7 @@
         + [pl.BlockSpec(memory_space=pl.ANY)] * 4,
         out_specs=(VM, VM),
         scratch_shapes=[
+            full(max(rows, grid.shape[0]), columns),
             half(2 * ESIDE * TILE, columns), half(src.size, columns),
             half(2 * DSIDE * TILE, columns), half(dec_src.size, columns),
             half(blocks, rows, columns), half(rows, w_qkv.shape[0]),
@@ -473,30 +520,22 @@
 
 
 def hand_on_kernel(*refs):
-    count = (len(refs) - 1) // 2
-    sems = refs[-1]
-    copies = []
-    for i in range(count):
-        half = refs[i].shape[0] // 2
-        for j in range(2):
-            here = pl.ds(j * half, half)
-            copies.append(
-                pltpu.make_async_copy(refs[i].at[here], refs[count + i].at[here], sems.at[2 * i + j])
-            )
-    for copy in copies:
-        copy.start()
-    for copy in copies:
-        copy.wait()
+    count = len(refs) // 2
+    for source, target in zip(refs[:count], refs[count:]):
+        target[...] = source[...]
 
 
 def hand_on(*arrays):
-    places = [pl.BlockSpec(memory_space=pl.ANY)] * len(arrays)
+    steps = 4
+    places = [
+        pl.BlockSpec((array.shape[0] // steps, array.shape[1]), lambda i: (i, 0)) for array in arrays
+    ]
     return pl.pallas_call(
         hand_on_kernel,
+        grid=(steps,),
         out_shape=tuple(jax.ShapeDtypeStruct(array.shape, array.dtype) for array in arrays),
         in_specs=places,
         out_specs=tuple(places),
-        scratch_shapes=[DMA((2 * len(arrays),))],
         compiler_params=pltpu.CompilerParams(vmem_limit_bytes=LIMIT),
         name="hand_on",
     )(*arrays)

time: 122 us -> 71.4 us (0.59)
  Pallas kernels: 120 us -> 69.9 us
    pallas_call x1, Pallas kernels: 48.8 us -> 3.62 us  [hand_on(): pl.pallas_call(hand_on_kernel, grid=(steps,), out_shape=tuple((jax.ShapeD...]
    pallas_call x1, Pallas kernels: 71.5 us -> 66.3 us  [layer(): pl.pallas_call(layer_kernel, out_shape=(jax.ShapeDtypeStruct((rows, colum...]
where the time goes in v3:
time: 71.4 us; the launch traced here: 71.2 us
  Pallas kernels  69.9 us (98%)
  between operations  1.29 us (2%)
    pallas_call x1, Pallas kernels, layer(): pl.pallas_call(layer_kernel, out_shape=(jax.ShapeDtypeStruct((rows, colum...  66.3 us
    pallas_call x1, Pallas kernels, hand_on(): pl.pallas_call(hand_on_kernel, grid=(steps,), out_shape=tuple((jax.ShapeD...  3.62 us

profile of v3, /device:TPU:0, one launch (start us, length us, event | category | flops | bytes accessed | tf_op | source)
XLA Modules:
  0.0 71.2 jit_solution(17679109515918834982)
XLA Ops:
  1.3 66.3 %encode_layer_decode.1 = (bf16[1024,256]{1,0:T(8,128)(2,1)}, bf16[2048,256]{1,0:T(8,128)(2,1)}) custom-call(s32[1]{0:T(128)S(6)} %copy.18.count_ref, s32[32,128]{1,0:T(8,128)} %bitcast.12, f32[32,128]{1,0:T(8,128)} %bitcast.13, s32[32,128]{1,0:T(8,128)} %bitcast.14, s32[48,128]{1,0:T(8,128)} %bitcast.9, f32[48,128]{1,0:T(8,128)} %bitcast.10, ...), custom_call_target="tpu_custom_call" | custom-call | tf_op jit(solution)/shard_map/encode_layer_decode/pallas_call | solution.py:487
  67.6 3.6 %hand_on.1 = (bf16[1024,256]{1,0:T(8,128)(2,1)}, bf16[2048,256]{1,0:T(8,128)(2,1)}) custom-call(bf16[1024,256]{1,0:T(8,128)(2,1)} %get-tuple-element.4.refs_0_, bf16[2048,256]{1,0:T(8,128)(2,1)} %get-tuple-element.5.refs_1_), custom_call_target="tpu_custom_call" | custom-call | tf_op jit(solution)/shard_map/hand_on/pallas_call | solution.py:533

commit v4 on v3

--- a/solution.py
+++ b/solution.py
@@ -20,19 +20,27 @@
 MESH = pl.DeviceIdType.MESH
 
 
-def turned(row):
-    return jnp.broadcast_to(row, (TILE, TILE)).T
+def turned(src, weight):
+    tiles = src.shape[0]
+    blank = jnp.zeros((TILE - 2 * tiles, TILE), jnp.float32)
+    both = jnp.concatenate([src.astype(jnp.float32), weight, blank], axis=0).T
+    return both[:, :tiles].astype(jnp.int32), both[:, tiles : 2 * tiles]
+
+
+def widened(columns, tile):
+    return jnp.broadcast_to(columns[:, tile : tile + 1], (TILE, TILE))
 
 
 def gather_group(src, weight, table, first=0):
     rows, columns = table.shape
     lane = lax.broadcasted_iota(jnp.int32, (TILE, rows), 1).astype(jnp.int16)
     picks, scales = [], []
-    for tile in range(src.shape[0]):
-        col = turned(src[tile : tile + 1] - first).astype(jnp.int16)
+    src, weight = turned(src - first, weight)
+    for tile in range(src.shape[1]):
+        col = widened(src, tile).astype(jnp.int16)
         col = jnp.concatenate([col] * (rows // TILE), axis=1)
         picks.append(jnp.where(lane == col, jnp.bfloat16(1), jnp.bfloat16(0)))
-        scale = turned(weight[tile : tile + 1])
+        scale = widened(weight, tile)
         scales.append(jnp.concatenate([scale] * (columns // TILE), axis=1))
     picked = jnp.dot(jnp.concatenate(picks, axis=0), table, preferred_element_type=jnp.float32)
     return (picked * jnp.concatenate(scales, axis=0)).astype(jnp.bfloat16)
@@ -302,12 +310,8 @@
     for load in loads:
         load.wait()
     forward(turn(0))
-    project(turn(0))
-    if chunks > 1:
-        forward(turn(1))
-    feed_forward(turn(0))
-
-    @pl.loop(1, chunks)
+
+    @pl.loop(0, chunks)
     def _(step):
         project(turn(step))
 
@@ -315,7 +319,11 @@
         def _():
             forward(turn(step + 1))
 
-    @pl.loop(1, chunks)
+        @pl.when(step < chunks // 2)
+        def _():
+            feed_forward(turn(step))
+
+    @pl.loop(chunks // 2, chunks)
     def _(step):
         feed_forward(turn(step))
 

time: 71.4 us -> 72.9 us (1.021)
  Pallas kernels: 69.9 us -> 70.8 us
    pallas_call x1, Pallas kernels: 66.3 us -> 67.2 us  [layer(): pl.pallas_call(layer_kernel, out_shape=(jax.ShapeDtypeStruct((rows, colum...]
where the time goes in v4:
time: 72.9 us; the launch traced here: 72.1 us
  Pallas kernels  70.8 us (97%)
  between operations  1.29 us (2%)
    pallas_call x1, Pallas kernels, layer(): pl.pallas_call(layer_kernel, out_shape=(jax.ShapeDtypeStruct((rows, colum...  67.2 us
    pallas_call x1, Pallas kernels, hand_on(): pl.pallas_call(hand_on_kernel, grid=(steps,), out_shape=tuple((jax.ShapeD...  3.62 us

profile of v4, /device:TPU:0, one launch (start us, length us, event | category | flops | bytes accessed | tf_op | source)
XLA Modules:
  0.0 72.1 jit_solution(5981086256542293916)
XLA Ops:
  1.3 67.2 %encode_layer_decode.1 = (bf16[1024,256]{1,0:T(8,128)(2,1)}, bf16[2048,256]{1,0:T(8,128)(2,1)}) custom-call(s32[1]{0:T(128)S(6)} %copy.18.count_ref, s32[32,128]{1,0:T(8,128)} %bitcast.12, f32[32,128]{1,0:T(8,128)} %bitcast.13, s32[32,128]{1,0:T(8,128)} %bitcast.14, s32[48,128]{1,0:T(8,128)} %bitcast.9, f32[48,128]{1,0:T(8,128)} %bitcast.10, ...), custom_call_target="tpu_custom_call" | custom-call | tf_op jit(solution)/shard_map/encode_layer_decode/pallas_call | solution.py:495
  68.5 3.6 %hand_on.1 = (bf16[1024,256]{1,0:T(8,128)(2,1)}, bf16[2048,256]{1,0:T(8,128)(2,1)}) custom-call(bf16[1024,256]{1,0:T(8,128)(2,1)} %get-tuple-element.4.refs_0_, bf16[2048,256]{1,0:T(8,128)(2,1)} %get-tuple-element.5.refs_1_), custom_call_target="tpu_custom_call" | custom-call | tf_op jit(solution)/shard_map/hand_on/pallas_call | solution.py:541
